TPU v7x, 128 devices: a whole 4x4x4 slice. The times are simulated.
128 devices in a mesh: gx: 4 (over x), gy: 32 (over z, y, core).
Axes of the slice: x: 4, y: 4, z: 4, core: 2. Of those that a mesh axis runs over, the one named last changes fastest.
Arguments:
- right_sides: bfloat16 [2048, 128, 256], P(('gx', 'gy')), may hold values from -6 to 6
- near_source: int32 [2048, 8], P(('gx', 'gy')), may hold values from 0 to 2047, as said below
- near_count: int32 [2048], P(('gx', 'gy')), may hold values from 2 to 8
- near_blocks: bfloat16 [2048, 8, 256, 256], P(('gx', 'gy')), may hold values from -0.125 to 0.125
- column_basis: bfloat16 [2048, 64, 256], P(('gx', 'gy')), may hold values from -0.375 to 0.375
- row_basis: bfloat16 [2048, 64, 256], P(('gx', 'gy')), may hold values from -0.75 to 0.75
- leaf_upward: bfloat16 [2048, 64, 64], P(('gx', 'gy')), may hold values from -0.25 to 0.25
- couple_source: int32 [2048, 8], P(('gx', 'gy')), may hold values from 0 to 2047, as said below
- couple_count: int32 [2048], P(('gx', 'gy')), may hold values from 1 to 8
- couple_blocks: bfloat16 [2048, 8, 64, 64], P(('gx', 'gy')), may hold values from -0.25 to 0.25
- mid_upward: bfloat16 [256, 64, 64], P(('gx', 'gy')), may hold values from -0.25 to 0.25
- mid_source: int32 [256, 4], P(('gx', 'gy')), may hold values from 0 to 255
- mid_blocks: bfloat16 [256, 4, 64, 64], P(('gx', 'gy')), may hold values from -0.375 to 0.375
- top_source: int32 [32, 4], replicated, may hold values from 0 to 31
- top_blocks: bfloat16 [32, 4, 64, 64], replicated, may hold values from -0.375 to 0.375
- mid_downward: bfloat16 [256, 64, 64], P(('gx', 'gy')), may hold values from -0.75 to 0.75
- leaf_downward: bfloat16 [2048, 64, 64], P(('gx', 'gy')), may hold values from -0.75 to 0.75
Outputs:
- product: bfloat16 [2048, 128, 256], P(('gx', 'gy'))
Inputs may be any that keep to these rules, and one draw needn't show every extreme that they name: `near_source`: every entry lies within 8 of its row's leaf in Morton order; slot 0 is the leaf itself; slot 1 of an even leaf l is max(l - 8, 0) and of an odd leaf min(l + 8, 2047). `couple_source`: every entry lies at distance 2 to 8 from its row's leaf in Morton order, or is the first or last leaf; slot 0 of an even leaf l is max(l - 8, 0) and of an odd leaf min(l + 8, 2047).
All inputs are finite; a program needn't handle non-finite values.
Results may differ from a plain program's by a relative error of at most 0.0065.
Values may be sent and summed in bfloat16 or wider, within the bound.
A program may use at most 128 MiB of HBM per device.

v0:
```python
import jax
import jax.numpy as jnp
from jax import lax
from jax.sharding import PartitionSpec as P

REACH = 8


HIGH = lax.Precision.HIGHEST


def padded(block, sides, width):
    for axis, dim in sides:
        count = lax.axis_size(axis)
        forward = [(i, i + 1) for i in range(count - 1)]
        backward = [(target, source) for source, target in forward]
        low = lax.ppermute(
            lax.slice_in_dim(block, block.shape[dim] - width, None, axis=dim), axis, forward
        )
        high = lax.ppermute(lax.slice_in_dim(block, 0, width, axis=dim), axis, backward)
        block = jnp.concatenate([low, block, high], axis=dim)
    return block


def local(
    right_sides,
    near_source,
    near_count,
    near_blocks,
    column_basis,
    row_basis,
    leaf_upward,
    couple_source,
    couple_count,
    couple_blocks,
    mid_upward,
    mid_source,
    mid_blocks,
    top_source,
    top_blocks,
    mid_downward,
    leaf_downward,
):
    leaf_dev = right_sides.shape[0]
    nrhs_local = right_sides.shape[1]
    rank_local = column_basis.shape[1]
    first_leaf = lax.axis_index(("gx", "gy")) * leaf_dev
    padded_sides = padded(right_sides, ((("gx", "gy"), 0),), REACH)
    skeleton = jnp.einsum(
        "lkp,lrp->lrk", column_basis, right_sides, preferred_element_type=jnp.float32
    ).astype(jnp.bfloat16)
    skeleton_all = padded(skeleton, ((("gx", "gy"), 0),), REACH)
    near_slots = jnp.arange(near_source.shape[1], dtype=jnp.int32)
    near_weight = (near_slots[None, :] < near_count[:, None]).astype(jnp.bfloat16)
    picked = padded_sides[near_source - first_leaf + REACH] * near_weight[:, :, None, None]
    near = jnp.einsum("lnrq,lnpq->lrp", picked, near_blocks, preferred_element_type=jnp.float32)
    couple_slots = jnp.arange(couple_source.shape[1], dtype=jnp.int32)
    couple_weight = (couple_slots[None, :] < couple_count[:, None]).astype(jnp.bfloat16)
    partners = skeleton_all[couple_source - first_leaf + REACH] * couple_weight[:, :, None, None]
    leaf_far = jnp.einsum(
        "lcij,lcrj->lri", couple_blocks, partners, preferred_element_type=jnp.float32
    )
    raised = jnp.einsum("lij,lrj->lri", leaf_upward, skeleton, preferred_element_type=jnp.float32)
    mid_skeleton = (
        raised.reshape(leaf_dev // 8, 8, nrhs_local, rank_local).sum(axis=1).astype(jnp.bfloat16)
    )
    lifted = jnp.einsum(
        "mij,mrj->mri", mid_upward, mid_skeleton, preferred_element_type=jnp.float32
    ).astype(jnp.bfloat16)
    every_mid, every_lift = (
        lax.all_gather(mid_skeleton, ("gx", "gy"), axis=0, tiled=True),
        lax.all_gather(lifted, ("gx", "gy"), axis=0, tiled=True),
    )
    mid_far = jnp.einsum(
        "mcij,mcrj->mri", mid_blocks, every_mid[mid_source], preferred_element_type=jnp.float32
    )
    top_skeleton = every_lift.astype(jnp.float32).reshape(-1, 8, nrhs_local, rank_local).sum(axis=1)
    own_top = lax.axis_index(("gx", "gy")) * (leaf_dev // 8) // 8
    top_row = lax.dynamic_index_in_dim(top_source, own_top, 0, keepdims=False)
    top_block = lax.dynamic_index_in_dim(top_blocks, own_top, 0, keepdims=False)
    top_far = jnp.einsum(
        "cij,crj->ri", top_block.astype(jnp.float32), top_skeleton[top_row], precision=HIGH
    )
    mid_local = mid_far + jnp.einsum(
        "mij,rj->mri", mid_downward.astype(jnp.float32), top_far, precision=HIGH
    )
    leaf_local = leaf_far + jnp.einsum(
        "lij,lrj->lri",
        leaf_downward.astype(jnp.float32),
        jnp.repeat(mid_local, 8, axis=0),
        precision=HIGH,
    )
    far = jnp.einsum(
        "lkp,lrk->lrp",
        row_basis,
        leaf_local.astype(jnp.bfloat16),
        preferred_element_type=jnp.float32,
    )
    return (near + far).astype(jnp.bfloat16)


def solution(mesh):
    placed = (
        P(("gx", "gy"), None, None),
        P(("gx", "gy"), None),
        P(("gx", "gy")),
        P(("gx", "gy"), None, None, None),
        P(("gx", "gy"), None, None),
        P(("gx", "gy"), None, None),
        P(("gx", "gy"), None, None),
        P(("gx", "gy"), None),
        P(("gx", "gy")),
        P(("gx", "gy"), None, None, None),
        P(("gx", "gy"), None, None),
        P(("gx", "gy"), None),
        P(("gx", "gy"), None, None, None),
        P(),
        P(),
        P(("gx", "gy"), None, None),
        P(("gx", "gy"), None, None),
    )
    return jax.shard_map(
        local, mesh=mesh, in_specs=placed, out_specs=P(("gx", "gy"), None, None), check_vma=False
    )
```

profile of v0, /device:TPU:2, one launch (start us, length us, event | category | flops | bytes accessed | tf_op | source)
XLA Modules:
  0.0 175.5 jit_solution(6324743820001020400)
XLA Ops:
  6.5 0.0 copy-start
  6.5 0.0 copy-start.1
  6.5 0.0 copy-start.5
  6.5 0.0 all-gather.5.cloned.1.call-start
  6.5 2.0 %convolution_convert_fusion = bf16[16,128,64]{1,2,0:T(8,128)(2,1)S(1)} fusion(bf16[16,128,256]{2,1,0:T(8,128)(2,1)} %param.17, bf16[16,64,256]{2,1,0:T(8,128)(2,1)} %param.21), kind=kOutput, calls=%fused_computation.17 | convolution fusion | flops 67239936 | bytes 1835008 | tf_op jit(solution)/shard_map/lkp,lrp->lrk/dot_general | solution.py:49
  8.5 0.0 copy-start.10
  8.6 0.0 copy-start.7
  8.6 0.0 copy-start.8
  8.6 0.0 copy-start.9
  8.6 1.2 bitcast_reduce_fusion
  9.8 0.0 copy-start.3
  9.8 0.0 copy-done.5
  9.8 0.7 convolution_convert_fusion.1
  10.5 0.0 all-gather.5.cloned.1.call-update
  10.6 0.0 all-gather.3.cloned.1.call-start
  10.6 0.0 copy-done.3
  10.6 0.7 all-gather.3.cloned.1.call-update
  11.3 0.7 fusion.31
  12.0 1.9 %collective-permute-start.2 = (bf16[8,128,64]{1,2,0:T(8,128)(2,1)}, bf16[8,128,64]{1,2,0:T(8,128)(2,1)}, u32[]{:S(2)}, u32[]{:S(2)}) collective-permute-start(bf16[8,128,64]{1,2,0:T(8,128)(2,1)} %get-tuple-element.7), channel_id=1, source_target_pairs={{0,1},{1,2},{2,3},{3,4},{4,5},{5,6},{6,7},{7,8},{8,9},{9,10},{10,1... | collective-permute-start | bytes 393224 | tf_op jit(solution)/shard_map/ppermute | solution.py:17
  13.9 7.9 %collective-permute-start.3 = (bf16[8,128,64]{1,2,0:T(8,128)(2,1)S(1)}, bf16[8,128,64]{1,2,0:T(8,128)(2,1)}, u32[]{:S(2)}, u32[]{:S(2)}) collective-permute-start(bf16[8,128,64]{1,2,0:T(8,128)(2,1)S(1)} %get-tuple-element.8), channel_id=1, source_target_pairs={{1,0},{2,1},{3,2},{4,3},{5,4},{6,5},{7,6},{8,7},{9,8},{10,9},{11,1... | collective-permute-start | bytes 393224 | tf_op jit(solution)/shard_map/ppermute | solution.py:20
  21.8 0.0 copy-done.1
  21.8 1.0 fusion.30
  22.8 1.9 %collective-permute-start = (bf16[8,128,256]{2,1,0:T(8,128)(2,1)}, bf16[8,128,256]{2,1,0:T(8,128)(2,1)S(1)}, u32[]{:S(2)}, u32[]{:S(2)}) collective-permute-start(bf16[8,128,256]{2,1,0:T(8,128)(2,1)} %get-tuple-element.5), channel_id=1, source_target_pairs={{0,1},{1,2},{2,3},{3,4},{4,5},{5,6},{6,7},{7,8},{8,9},{9,10},{10,1... | collective-permute-start | bytes 1572872 | tf_op jit(solution)/shard_map/ppermute | solution.py:17
  24.7 7.9 %collective-permute-start.1 = (bf16[8,128,256]{2,1,0:T(8,128)(2,1)}, bf16[8,128,256]{2,1,0:T(8,128)(2,1)}, u32[]{:S(2)}, u32[]{:S(2)}) collective-permute-start(bf16[8,128,256]{2,1,0:T(8,128)(2,1)} %get-tuple-element.6), channel_id=1, source_target_pairs={{1,0},{2,1},{3,2},{4,3},{5,4},{6,5},{7,6},{8,7},{9,8},{10,9},{11,1... | collective-permute-start | bytes 1572872 | tf_op jit(solution)/shard_map/ppermute | solution.py:20
  32.6 0.0 copy-done.10
  32.6 0.1 reshape.108
  32.7 0.0 copy-done.7
  32.7 0.0 copy-done.8
  32.7 0.1 copy.25
  32.8 0.1 reshape.100
  32.9 0.0 copy-done.9
  32.9 0.2 dynamic-slice_reduce_fusion
  33.1 0.6 pad_clamp_fusion
  33.7 0.7 fusion.27
  34.4 1.3 fusion.26
  35.8 0.1 copy.24
  35.8 0.1 reshape.92
  35.9 0.0 collective-permute-done.2
  36.0 0.0 collective-permute-done.3
  36.0 1.0 pad_maximum_fusion.1
  37.0 2.1 %gather_fusion.1 = bf16[128,128,64]{1,2,0:T(8,128)(2,1)} fusion(bf16[32,128,64]{1,2,0:T(8,128)(2,1)S(1)} %pad_maximum_fusion.1, s32[1024]{0:T(1024)S(1)} %pad_clamp_fusion.2), kind=kCustom, calls=%fused_computation.1 | custom fusion | bytes 4194816 | tf_op jit(solution)/shard_map/gather | solution.py:59
  39.1 0.0 collective-permute-done
  39.1 0.5 collective-permute-done.1
  39.6 2.9 %pad_maximum_fusion = bf16[32,128,256]{2,1,0:T(8,128)(2,1)} fusion(bf16[8,128,256]{2,1,0:T(8,128)(2,1)} %collective-permute-done.1, bf16[16,128,256]{2,1,0:T(8,128)(2,1)} %param.17, bf16[8,128,256]{2,1,0:T(8,128)(2,1)S(1)} %collective-permute-done), kind=kLoop, calls=%fused_computation.8 | loop fusion | flops 2097152 | bytes 4194304 | tf_op jit(solution)/shard_map/concatenate | solution.py:21
  42.6 8.2 %gather_fusion = bf16[128,128,256]{2,1,0:T(8,128)(2,1)} fusion(bf16[32,128,256]{2,1,0:T(8,128)(2,1)} %pad_maximum_fusion, s32[1024]{0:T(1024)S(1)} %pad_clamp_fusion.3), kind=kCustom, calls=%fused_computation | custom fusion | bytes 16777728 | tf_op jit(solution)/shard_map/gather | solution.py:55
  50.8 28.0 %all-gather.5.cloned.1.call-done = bf16[256,128,64]{1,2,0:T(8,128)(2,1)} async-done(((bf16[2,128,64]{1,2,0:T(8,128)(2,1)}), bf16[256,128,64]{1,2,0:T(8,128)(2,1)}) %all-gather.5.cloned.1.call-update) | async-done | bytes 4194320 | tf_op jit(solution)/shard_map/all_gather | solution.py:72
  78.8 3.2 %convert_reduce_fusion = f32[32,128,64]{1,2,0:T(8,128)S(1)} fusion(bf16[256,128,64]{1,2,0:T(8,128)(2,1)} %all-gather.5.cloned.1.call-done), kind=kLoop, calls=%fused_computation.4 | loop fusion | flops 3932160 | bytes 5242880 | tf_op jit(solution)/shard_map/reduce_sum | solution.py:77
  82.0 0.0 copy-start.4
  82.0 0.8 gather_fusion.3
  82.8 0.0 copy-start.2
  82.8 1.1 fusion.23
  83.9 62.5 %all-gather.3.cloned.1.call-done = bf16[256,128,64]{1,2,0:T(8,128)(2,1)} async-done(((bf16[2,128,64]{1,2,0:T(8,128)(2,1)}), bf16[256,128,64]{1,2,0:T(8,128)(2,1)}) %all-gather.3.cloned.1.call-update) | async-done | bytes 4194320 | tf_op jit(solution)/shard_map/all_gather | solution.py:71
  146.4 2.8 %gather_fusion.2 = bf16[8,128,64]{1,2,0:T(8,128)(2,1)S(1)} fusion(bf16[256,128,64]{1,2,0:T(8,128)(2,1)} %all-gather.3.cloned.1.call-done, s32[1024]{0:T(1024)S(1)} %pad_clamp_fusion.1), kind=kCustom, calls=%fused_computation.2 | custom fusion | bytes 262176 | tf_op jit(solution)/shard_map/gather | solution.py:75
  149.2 1.1 convolution_bitcast_fusion
  150.3 0.9 fusion.20
  151.3 0.0 copy-done.4
  151.3 0.4 fusion.32
  151.7 0.0 copy-done
  151.7 0.0 copy-done.2
  151.7 0.0 copy-start.6
  151.7 4.1 %fusion.18 = f32[16,128,256]{2,1,0:T(8,128)} fusion(bf16[16,64,256]{2,1,0:T(8,128)(2,1)S(1)} %copy-done.2, f32[16,128,64]{1,2,0:T(8,128)S(1)} %fusion.32, bf16[16,8,64,64]{3,2,1,0:T(8,128)(2,1)S(1)} %copy-done, bf16[16,8,128,64]{2,3,1,0:T(8,128)(2,1)} %bitcast.54, bf16[16,8]{1,0:T(8,128)(2,1)S(1)} %fusion.27), kind=kOutput, calls=%fused_computation.16 | convolution fusion | flops 205783040 | bytes 6291712 | tf_op jit(solution)/shard_map/lkp,lrk->lrp/dot_general | solution.py:93
  155.9 0.0 copy-done.6
  155.9 12.8 %fusion.3 = bf16[16,128,256]{2,1,0:T(8,128)(2,1)} fusion(f32[16,128,256]{2,1,0:T(8,128)} %fusion.18, bf16[16,8,256,256]{3,2,1,0:T(8,128)(2,1)} %param.20, bf16[16,8,128,256]{3,2,1,0:T(8,128)(2,1)} %bitcast.55, bf16[16,8]{1,0:T(8,128)(2,1)S(1)} %copy-done.6), kind=kOutput, calls=%fused_computation.10 | convolution fusion | flops 2152726528 | bytes 28311808 | tf_op jit(solution)/shard_map/lnrq,lnpq->lrp/dot_general | solution.py:56
  (7 shorter events, 0.1 us)
Async XLA Ops:
  6.5 145.1 %copy-start = (bf16[16,8,64,64]{3,2,1,0:T(8,128)(2,1)S(1)}, bf16[16,8,64,64]{3,2,1,0:T(8,128)(2,1)}, u32[]{:S(2)}) copy-start(bf16[16,8,64,64]{3,2,1,0:T(8,128)(2,1)} %param.26) | copy-start | bytes 3145732
  6.5 15.2 %copy-start.1 = (bf16[16,128,256]{2,1,0:T(8,128)(2,1)S(1)}, bf16[16,128,256]{2,1,0:T(8,128)(2,1)}, u32[]{:S(2)}) copy-start(bf16[16,128,256]{2,1,0:T(8,128)(2,1)} %param.17) | copy-start | bytes 3145732
  6.5 3.2 %copy-start.5 = (bf16[2,64,64]{2,1,0:T(8,128)(2,1)S(1)}, bf16[2,64,64]{2,1,0:T(8,128)(2,1)}, u32[]{:S(2)}) copy-start(bf16[2,64,64]{2,1,0:T(8,128)(2,1)} %param.27) | copy-start | bytes 49156
  6.5 72.2 %all-gather.5.cloned.1.call-start = ((), (), s32[]{:S(2)}) async-start(), calls=%async_computation.1 | async-start | bytes 4227072 | tf_op jit(solution)/shard_map/all_gather | solution.py:72
  8.5 24.1 %copy-start.10 = (s32[2,4]{1,0:T(2,128)S(1)}, s32[2,4]{1,0:T(2,128)}, u32[]{:S(2)}) copy-start(s32[2,4]{1,0:T(2,128)} %param.28) | copy-start | bytes 100
  8.6 24.2 %copy-start.7 = (s32[16,8]{0,1:T(8,128)S(1)}, s32[16,8]{0,1:T(8,128)}, u32[]{:S(2)}) copy-start(s32[16,8]{0,1:T(8,128)} %param.24) | copy-start | bytes 1540
  8.6 24.1 %copy-start.8 = (s32[16,8]{0,1:T(8,128)S(1)}, s32[16,8]{0,1:T(8,128)}, u32[]{:S(2)}) copy-start(s32[16,8]{0,1:T(8,128)} %param.18) | copy-start | bytes 1540
  8.6 24.3 %copy-start.9 = (s32[32,4]{0,1:T(4,128)S(1)}, s32[32,4]{0,1:T(4,128)}, u32[]{:S(2)}) copy-start(s32[32,4]{0,1:T(4,128)} %param.30) | copy-start | bytes 1540
  9.8 0.8 copy-start.3
  10.6 135.8 %all-gather.3.cloned.1.call-start = ((), (), s32[]{:S(2)}) async-start(), calls=%async_computation | async-start | bytes 4227072 | tf_op jit(solution)/shard_map/all_gather | solution.py:71
  12.0 24.0 %collective-permute-start.2 = (bf16[8,128,64]{1,2,0:T(8,128)(2,1)}, bf16[8,128,64]{1,2,0:T(8,128)(2,1)}, u32[]{:S(2)}, u32[]{:S(2)}) collective-permute-start(bf16[8,128,64]{1,2,0:T(8,128)(2,1)} %get-tuple-element.7), channel_id=1, source_target_pairs={{0,1},{1,2},{2,3},{3,4},{4,5},{5,6},{6,7},{7,8},{8,9},{9,10},{10,1... | collective-permute-start | bytes 393224 | tf_op jit(solution)/shard_map/ppermute | solution.py:17
  13.9 22.1 %collective-permute-start.3 = (bf16[8,128,64]{1,2,0:T(8,128)(2,1)S(1)}, bf16[8,128,64]{1,2,0:T(8,128)(2,1)}, u32[]{:S(2)}, u32[]{:S(2)}) collective-permute-start(bf16[8,128,64]{1,2,0:T(8,128)(2,1)S(1)} %get-tuple-element.8), channel_id=1, source_target_pairs={{1,0},{2,1},{3,2},{4,3},{5,4},{6,5},{7,6},{8,7},{9,8},{10,9},{11,1... | collective-permute-start | bytes 393224 | tf_op jit(solution)/shard_map/ppermute | solution.py:20
  22.8 16.3 %collective-permute-start = (bf16[8,128,256]{2,1,0:T(8,128)(2,1)}, bf16[8,128,256]{2,1,0:T(8,128)(2,1)S(1)}, u32[]{:S(2)}, u32[]{:S(2)}) collective-permute-start(bf16[8,128,256]{2,1,0:T(8,128)(2,1)} %get-tuple-element.5), channel_id=1, source_target_pairs={{0,1},{1,2},{2,3},{3,4},{4,5},{5,6},{6,7},{7,8},{8,9},{9,10},{10,1... | collective-permute-start | bytes 1572872 | tf_op jit(solution)/shard_map/ppermute | solution.py:17
  24.7 14.9 %collective-permute-start.1 = (bf16[8,128,256]{2,1,0:T(8,128)(2,1)}, bf16[8,128,256]{2,1,0:T(8,128)(2,1)}, u32[]{:S(2)}, u32[]{:S(2)}) collective-permute-start(bf16[8,128,256]{2,1,0:T(8,128)(2,1)} %get-tuple-element.6), channel_id=1, source_target_pairs={{1,0},{2,1},{3,2},{4,3},{5,4},{6,5},{7,6},{8,7},{9,8},{10,9},{11,1... | collective-permute-start | bytes 1572872 | tf_op jit(solution)/shard_map/ppermute | solution.py:20
  82.0 69.3 %copy-start.4 = (bf16[16,64,64]{2,1,0:T(8,128)(2,1)S(1)}, bf16[16,64,64]{2,1,0:T(8,128)(2,1)}, u32[]{:S(2)}) copy-start(bf16[16,64,64]{2,1,0:T(8,128)(2,1)} %param.33) | copy-start | bytes 393220
  82.8 68.9 %copy-start.2 = (bf16[16,64,256]{2,1,0:T(8,128)(2,1)S(1)}, bf16[16,64,256]{2,1,0:T(8,128)(2,1)}, u32[]{:S(2)}) copy-start(bf16[16,64,256]{2,1,0:T(8,128)(2,1)} %param.22) | copy-start | bytes 1572868
  151.7 4.2 %copy-start.6 = (bf16[16,8]{1,0:T(8,128)(2,1)S(1)}, bf16[16,8]{1,0:T(8,128)(2,1)}, u32[]{:S(2)}) copy-start(bf16[16,8]{1,0:T(8,128)(2,1)} %fusion.26) | copy-start | bytes 772
Sparse Core Ops, SparseCore 0:
  10.7 68.0 all-gather.4
  81.9 64.4 all-gather.2
where the time goes:
time: 179 us; the launch traced here: 176 us
  waiting for transfers between devices  91.7 us (51%)
  matrix products  24.4 us (14%)
  starting transfers between devices  19.6 us (11%)
  local copies, waits for them, and re-layouts  16.3 us (9%)
  between operations  13.7 us (8%)
  other arithmetic  9.83 us (5%)
    all_gather x1, waiting for transfers between devices, local(): lax.all_gather(mid_skeleton, ('gx', 'gy'), axis=0, tiled=True)  62.5 us
    all_gather x1, waiting for transfers between devices, local(): lax.all_gather(lifted, ('gx', 'gy'), axis=0, tiled=True)  28 us
    ppermute x2, starting transfers between devices, padded(): lax.ppermute(lax.slice_in_dim(block, 0, width, axis=dim), axis, backward)  15.7 us
    dot_general x1, matrix products, local(): jnp.einsum('lnrq,lnpq->lrp', picked, near_blocks, preferred_element_type=...  12.8 us
    gather x1, local copies, waits for them, and re-layouts, local(): padded_sides[near_source - first_leaf + REACH]  8.19 us
    dot_general x1, matrix products, local(): jnp.einsum('lkp,lrk->lrp', row_basis, leaf_local.astype(jnp.bfloat16), pr...  4.15 us
    concatenate x2, other arithmetic, padded(): block = jnp.concatenate([low, block, high], axis=dim)  3.98 us
    ppermute x2, starting transfers between devices, padded(): lax.ppermute(lax.slice_in_dim(block, block.shape[dim] - width, None, axis...  3.82 us
  transfers between devices with their start and end apart: 6, of which 3 were waited for; matrix products, arithmetic and copies ran while one was open for 14% of the time, Pallas kernels for 0%

commit v1 on v0

v1 whole, which is shorter than its diff:
```python
import functools

import jax
import jax.numpy as jnp
from jax import lax
from jax.experimental import pallas as pl
from jax.experimental.pallas import tpu as pltpu
from jax.sharding import PartitionSpec as P

MESH = pl.DeviceIdType.MESH
F32 = jnp.float32
BF16 = jnp.bfloat16
LINE = 4
PER = 10


def dot(a, b):
    return lax.dot_general(a, b, (((1,), (0,)), ((), ())), preferred_element_type=F32)


def dot_nt(a, b):
    return lax.dot_general(a, b, (((1,), (1,)), ((), ())), preferred_element_type=F32)


def dot_tn(a, b):
    return lax.dot_general(a, b, (((0,), (0,)), ((), ())), preferred_element_type=F32)


def kernel(
    rs_hbm, ns_hbm, nc_hbm, nb_hbm, cb_hbm, rb_hbm, lu_hbm, cs_hbm, cc_hbm, cp_hbm,
    mu_hbm, ms_hbm, mb_hbm, ts_hbm, tb_hbm, md_hbm, ld_hbm,
    out_hbm,
    rsw, nb, cb, rb, lu, cp, mu, mb, tb, md, ld,
    ns, nc, cs, cc, ts, mss, msv,
    skw, ust, cst, tst, qown, qin, qfull, mown, g1, g2, psend, precv,
    leaf_far, acc, outv,
    load_sem, nb_sem, out_sem,
    halo_send, halo_recv, skel_send, skel_recv, q_send, q_recv, i_send, i_recv,
    y_send, y_recv, g_send, g_recv, p_send, p_recv,
):
    x = lax.axis_index("gx")
    gy = lax.axis_index("gy")
    z = gy // 8
    y = (gy // 2) % 4
    c = gy % 2
    first = c == 0
    me = x * 32 + gy
    v = jnp.where(first, x, z)
    w = jnp.where(first, z, x)

    def on_line(place, core):
        return (jnp.where(first, place, x), jnp.where(first, z, place) * 8 + y * 2 + core)

    def on_gather(place):
        return (jnp.where(first, x, place), jnp.where(first, place, z) * 8 + y * 2 + c)

    def ring(step):
        d = lax.rem(me + step + 128, 128)
        return (d // 32, lax.rem(d, 32))

    sibling = (x, z * 8 + y * 2 + 1 - c)
    y_dev = lambda k: (x, z * 8 + lax.rem(y + k, 4) * 2 + c)
    x_dev = lambda k, core: (lax.rem(x + k, 4), z * 8 + y * 2 + core)
    z_dev = lambda k, core: (x, lax.rem(z + k, 4) * 8 + y * 2 + core)

    loads = {}

    def load(name, src, dst):
        loads[name] = pltpu.make_async_copy(src, dst, load_sem.at[len(loads)])
        loads[name].start()

    load("mb", mb_hbm, mb)
    load("md", md_hbm, md)
    load("rs", rs_hbm, rsw.at[pl.ds(8, 16)])
    load("cb", cb_hbm, cb)
    load("lu", lu_hbm, lu)
    load("mu", mu_hbm, mu)
    load("ns", ns_hbm, ns)
    load("nc", nc_hbm, nc)
    load("cs", cs_hbm, cs)
    load("cc", cc_hbm, cc)
    load("ts", ts_hbm, ts)
    load("ms", ms_hbm, msv.at[2 * v + c])
    for place in range(LINE):
        top = jnp.where(first, place * 8 + z * 2, x * 8 + place * 2) + y // 2
        load(f"tb{place}", tb_hbm.at[top], tb.at[place])
    load("cp", cp_hbm, cp)
    load("rb", rb_hbm, rb)
    load("ld", ld_hbm, ld)

    barrier = pltpu.get_barrier_semaphore()
    peers = [ring(1), ring(-1), sibling]
    for k in range(1, LINE):
        peers += [y_dev(k), x_dev(k, 0), x_dev(k, 1), z_dev(k, 0), z_dev(k, 1)]
    for peer in peers:
        pl.semaphore_signal(barrier, inc=1, device_id=peer, device_id_type=MESH)

    loads["mb"].wait()
    loads["md"].wait()
    for m in range(2):
        qown[:, 256 * m : 256 * m + 256] = jnp.concatenate([mb[m, k] for k in range(4)], axis=1)
    qown[:, 512:] = jnp.concatenate([md[0], md[1]], axis=1)
    loads["rs"].wait()
    pl.semaphore_wait(barrier, len(peers))

    def send(src, dst, send_sem, recv_sem, device):
        copy = pltpu.make_async_remote_copy(
            src_ref=src, dst_ref=dst, send_sem=send_sem, recv_sem=recv_sem,
            device_id=device, device_id_type=MESH,
        )
        copy.start()
        return copy

    sent = []
    halo = [
        send(rsw.at[pl.ds(8, 8)], rsw.at[pl.ds(24, 8)], halo_send.at[0], halo_recv.at[0], ring(-1)),
        send(rsw.at[pl.ds(16, 8)], rsw.at[pl.ds(0, 8)], halo_send.at[1], halo_recv.at[1], ring(1)),
    ]
    sent += halo
    slot0, slot1 = x * 2 + c, z * 2 + c
    for k in range(1, LINE):
        for core, device, slot in ((0, x_dev(k, 0), slot0), (1, z_dev(k, 1), slot1)):
            at = 2 * (k - 1) + core
            sem = 2 * (k - 1) + c
            sent.append(send(qown, qin.at[slot], q_send.at[at], q_recv.at[sem], device))
            sent.append(send(ms_hbm, msv.at[slot], i_send.at[at], i_recv.at[sem], device))
    slot = jnp.where(first, slot1, slot0)
    sent.append(send(qown, qin.at[slot], q_send.at[6], q_recv.at[6], sibling))
    sent.append(send(ms_hbm, msv.at[slot], i_send.at[6], i_recv.at[6], sibling))
    mine = 2 * v + c
    qin[mine] = qown[...]

    loads["cb"].wait()
    for t in range(16):
        pltpu.make_async_copy(nb_hbm.at[t], nb.at[t], nb_sem.at[t]).start()

    for l in range(16):
        skw[8 + l] = dot_nt(cb[l], rsw[8 + l]).astype(BF16)
    skel = [
        send(skw.at[pl.ds(8, 8)], skw.at[pl.ds(24, 8)], skel_send.at[0], skel_recv.at[0], ring(-1)),
        send(skw.at[pl.ds(16, 8)], skw.at[pl.ds(0, 8)], skel_send.at[1], skel_recv.at[1], ring(1)),
    ]
    sent += skel
    loads["lu"].wait()
    loads["mu"].wait()
    lift = None
    for m in range(2):
        upward = jnp.concatenate([lu[8 * m + l] for l in range(8)], axis=1)
        raised = dot(upward, skw[8 + 8 * m : 16 + 8 * m].reshape(512, 128)).astype(BF16)
        mown[m] = raised
        lifted = dot(mu[m], raised).astype(BF16).astype(F32)
        lift = lifted if lift is None else lift + lifted
    mown[2] = lift.astype(BF16)
    g1[y] = mown[...]
    gather1 = [send(mown, g1.at[y], y_send.at[k - 1], y_recv.at[k - 1], y_dev(k)) for k in range(1, LINE)]
    sent += gather1

    for place in range(LINE):
        loads[f"tb{place}"].wait()
        tst[place] = jnp.concatenate([tb[place, k] for k in range(4)], axis=1)
    loads["cp"].wait()
    for t in range(16):
        cst[t] = jnp.concatenate([cp[t, k] for k in range(8)], axis=1)

    for copy in gather1:
        copy.wait_recv()
    for p in range(4):
        for m in range(2):
            g2[w * PER + 2 * p + m] = g1[p, m]
    for h in range(2):
        g2[w * PER + 8 + h] = (g1[2 * h, 2].astype(F32) + g1[2 * h + 1, 2].astype(F32)).astype(BF16)
    part = g2.at[pl.ds(w * PER, PER)]
    gather2 = [
        send(part, part, g_send.at[k - 1], g_recv.at[k - 1], on_gather(lax.rem(w + k, LINE)))
        for k in range(1, LINE)
    ]
    sent += gather2

    for at in range(7):
        pltpu.make_async_remote_copy(
            src_ref=qown, dst_ref=qin.at[0], send_sem=q_send.at[at], recv_sem=q_recv.at[at],
            device_id=sibling, device_id_type=MESH,
        ).wait_recv()
        pltpu.make_async_remote_copy(
            src_ref=ms_hbm, dst_ref=msv.at[0], send_sem=i_send.at[at], recv_sem=i_recv.at[at],
            device_id=sibling, device_id_type=MESH,
        ).wait_recv()
    loads["ms"].wait()
    loads["ts"].wait()
    tables = pltpu.make_async_copy(msv, mss, out_sem.at[0])
    tables.start()
    lane = lax.broadcasted_iota(jnp.int32, (64, 128), 1)
    for s in range(8):
        down = qin[s, :, 512:]
        zero = jnp.zeros_like(down)
        both = jnp.concatenate([jnp.where(lane < 64, down, zero), jnp.where(lane < 64, zero, down)], axis=0)
        folded = dot(both, jnp.concatenate([tst[s // 2], tst[s // 2]], axis=0)).astype(BF16)
        for m in range(2):
            qfull[s, m, :, :256] = qin[s, :, 256 * m : 256 * m + 256]
            qfull[s, m, :, 256:] = folded[64 * m : 64 * m + 64]
    tables.wait()

    for copy in skel:
        copy.wait_recv()
    loads["cs"].wait()
    loads["cc"].wait()
    base = me * 16 - 8
    for t in range(16):
        rows = []
        for k in range(8):
            row = skw[jnp.clip(cs[k, t] - base, 0, 31)]
            rows.append(jnp.where(k < cc[t], row, jnp.zeros_like(row)))
        leaf_far[t] = dot(cst[t], jnp.concatenate(rows, axis=0))

    for copy in gather2:
        copy.wait_recv()

    def mid_row(m):
        dev = m // 2
        mx, mz, my, mc = dev // 32, (dev // 8) % 4, (dev // 2) % 4, dev % 2
        held = (mc == c) & (jnp.where(first, mx, mz) == v)
        row = g2[jnp.where(first, mz, mx) * PER + my * 2 + m % 2]
        return jnp.where(held, row, jnp.zeros_like(row))

    def top_row(n):
        nx, nz = n // 8, (n // 2) % 4
        row = g2[jnp.where(first, nz, nx) * PER + 8 + n % 2]
        return jnp.where(jnp.where(first, nx, nz) == v, row, jnp.zeros_like(row))

    for place in range(LINE):
        top = jnp.where(first, place * 8 + z * 2, x * 8 + place * 2) + y // 2
        tops = [top_row(ts[k, top]) for k in range(4)]
        for core in range(2):
            s = 2 * place + core
            for m in range(2):
                rows = [mid_row(mss[s, m, k]) for k in range(4)]
                psend[s, m] = dot(qfull[s, m], jnp.concatenate(rows + tops, axis=0)).astype(BF16)
    for k in range(1, LINE):
        place = lax.rem(v + k, LINE)
        for core in range(2):
            at = 2 * (k - 1) + core
            sent.append(
                send(psend.at[2 * place + core], precv.at[4 * c + v], p_send.at[at], p_recv.at[3 * c + k - 1],
                     on_line(place, core))
            )
    sent.append(send(psend.at[2 * v + 1 - c], precv.at[4 * c + v], p_send.at[6], p_recv.at[6], sibling))
    precv[4 * c + v] = psend[mine]

    for copy in halo:
        copy.wait_recv()
    loads["ns"].wait()
    loads["nc"].wait()

    def near(t, carry):
        pltpu.make_async_copy(nb_hbm.at[t], nb.at[t], nb_sem.at[t]).wait()
        total = jnp.zeros((128, 256), F32)
        for k in range(8):
            side = rsw[jnp.clip(ns[k, t] - base, 0, 31)]
            total += dot_nt(jnp.where(k < nc[t], side, jnp.zeros_like(side)), nb[t, k])
        acc[t] = total
        return carry

    lax.fori_loop(0, 16, near, 0)

    loads["ld"].wait()
    loads["rb"].wait()
    for at in range(7):
        pltpu.make_async_remote_copy(
            src_ref=psend.at[0], dst_ref=precv.at[0], send_sem=p_send.at[at], recv_sem=p_recv.at[at],
            device_id=sibling, device_id_type=MESH,
        ).wait_recv()
    copies = []
    for m in range(2):
        total = precv[0, m].astype(F32)
        for s in range(1, 8):
            total += precv[s, m].astype(F32)
        lowered = dot(ld[8 * m : 8 * m + 8].reshape(512, 64), total.astype(BF16))
        for l in range(8):
            t = 8 * m + l
            local = (leaf_far[t] + lowered[64 * l : 64 * l + 64]).astype(BF16)
            outv[t] = (acc[t] + dot_tn(local, rb[t])).astype(BF16)
        copy = pltpu.make_async_copy(
            outv.at[pl.ds(8 * m, 8)], out_hbm.at[pl.ds(8 * m, 8)], out_sem.at[1 + m]
        )
        copy.start()
        copies.append(copy)
    for copy in sent:
        copy.wait_send()
    for copy in copies:
        copy.wait()


def local(*args):
    args = list(args)
    for at in (1, 7, 13):
        args[at] = args[at].T
    vmem = pltpu.VMEM
    smem = pltpu.SMEM
    dma = pltpu.SemaphoreType.DMA
    scratch = [
        vmem((32, 128, 256), BF16),
        vmem((16, 8, 256, 256), BF16),
        vmem((16, 64, 256), BF16),
        vmem((16, 64, 256), BF16),
        vmem((16, 64, 64), BF16),
        vmem((16, 8, 64, 64), BF16),
        vmem((2, 64, 64), BF16),
        vmem((2, 4, 64, 64), BF16),
        vmem((4, 4, 64, 64), BF16),
        vmem((2, 64, 64), BF16),
        vmem((16, 64, 64), BF16),
        smem((8, 16), jnp.int32),
        smem((16,), jnp.int32),
        smem((8, 16), jnp.int32),
        smem((16,), jnp.int32),
        smem((4, 32), jnp.int32),
        smem((8, 2, 4), jnp.int32),
        vmem((8, 2, 4), jnp.int32),
        vmem((32, 64, 128), BF16),
        vmem((2, 64, 512), BF16),
        vmem((16, 64, 512), BF16),
        vmem((4, 64, 256), BF16),
        vmem((64, 640), BF16),
        vmem((8, 64, 640), BF16),
        vmem((8, 2, 64, 512), BF16),
        vmem((3, 64, 128), BF16),
        vmem((4, 3, 64, 128), BF16),
        vmem((4 * PER, 64, 128), BF16),
        vmem((8, 2, 64, 128), BF16),
        vmem((8, 2, 64, 128), BF16),
        vmem((16, 64, 128), F32),
        vmem((16, 128, 256), F32),
        vmem((16, 128, 256), BF16),
        dma((20,)), dma((16,)), dma((3,)),
        dma((2,)), dma((2,)), dma((2,)), dma((2,)),
        dma((7,)), dma((7,)), dma((7,)), dma((7,)),
        dma((3,)), dma((3,)), dma((3,)), dma((3,)),
        dma((7,)), dma((7,)),
    ]
    return pl.pallas_call(
        kernel,
        out_shape=jax.ShapeDtypeStruct((16, 128, 256), BF16),
        in_specs=[pl.BlockSpec(memory_space=pl.ANY)] * len(args),
        out_specs=pl.BlockSpec(memory_space=pl.ANY),
        scratch_shapes=scratch,
        compiler_params=pltpu.CompilerParams(
            collective_id=0, has_side_effects=True, vmem_limit_bytes=56 * 1024 * 1024
        ),
    )(*args)


def solution(mesh):
    both = ("gx", "gy")
    placed = [P(both)] * 17
    placed[13] = placed[14] = P()
    return jax.shard_map(
        local, mesh=mesh, in_specs=tuple(placed), out_specs=P(both), check_vma=False
    )
```

time: 179 us -> 40.2 us (0.22)
  the two profiles are of different devices: /device:TPU:2 before, /device:TPU:1 now
where the time goes in v1:
time: 40.2 us; the launch traced here: 40.1 us
  Pallas kernels  37.8 us (94%)
  local copies, waits for them, and re-layouts  2.29 us (6%)
    pallas_call x1, Pallas kernels, local(): pl.pallas_call(kernel, out_shape=jax.ShapeDtypeStruct((16, 128, 256), BF1...  37.8 us
    unnamed x1, local copies, waits for them, and re-layouts  2.29 us

profile of v1, /device:TPU:1, one launch (start us, length us, event | category | flops | bytes accessed | tf_op | source)
XLA Modules:
  0.0 40.1 jit_solution(6020959399801939131)
XLA Ops:
  0.0 37.8 %shard_map.163 = bf16[16,128,256]{2,1,0:T(8,128)(2,1)} custom-call(bf16[16,128,256]{2,1,0:T(8,128)(2,1)} %rs_hbm.1, s32[8,16]{1,0:T(8,128)} %bitcast.3, s32[16]{0:T(128)} %nc_hbm.1, bf16[16,8,256,256]{3,2,1,0:T(8,128)(2,1)} %nb_hbm.1, bf16[16,64,256]{2,1,0:T(8,128)(2,1)} %cb_hbm.1, bf16[16,64,256]{2,1,0:T(8,128)(2,1)} %rb_hbm.1, bf16[16,64,64]{2,1,0:T(8,128)(2,1)} %lu_hbm.1, ...), custom_call_target="tpu_custom_call" | custom-call | tf_op jit(solution)/shard_map/pallas_call | solution.py:340
  37.8 2.3 %copy.19 = bf16[16,128,256]{2,1,0:T(8,128)(2,1)} copy(bf16[16,128,256]{2,1,0:T(8,128)(2,1)} %shard_map.163) | data formatting | bytes 2097152

commit v2 on v1

v2 whole, which is shorter than its diff:
```python
import functools

import jax
import jax.numpy as jnp
from jax import lax
from jax.experimental import pallas as pl
from jax.experimental.pallas import tpu as pltpu
from jax.sharding import PartitionSpec as P

MESH = pl.DeviceIdType.MESH
F32 = jnp.float32
BF16 = jnp.bfloat16
LINE = 4
PER = 10


def dot(a, b):
    return lax.dot_general(a, b, (((1,), (0,)), ((), ())), preferred_element_type=F32)


def dot_nt(a, b):
    return lax.dot_general(a, b, (((1,), (1,)), ((), ())), preferred_element_type=F32)


def dot_tn(a, b):
    return lax.dot_general(a, b, (((0,), (0,)), ((), ())), preferred_element_type=F32)


def kernel(
    rs_hbm, ns_hbm, nc_hbm, nb_hbm, cb_hbm, rb_hbm, lu_hbm, cs_hbm, cc_hbm, cp_hbm,
    mu_hbm, ms_hbm, mb_hbm, ts_hbm, tb_hbm, md_hbm, ld_hbm,
    out,
    rlo, rhi, nb, cb, rb, lu, cp, mu, mb, tb, md, ld,
    ns, nc, cs, cc, ts, mss, mix, tix, msv,
    skw, ust, cst, tst, qown, qin, qfull, mown, g1, g2, psend, precv,
    leaf_far, acc,
    load_sem, nb_sem, out_sem,
    halo_send, halo_recv, skel_send, skel_recv, q_send, q_recv, i_send, i_recv,
    y_send, y_recv, g_send, g_recv, p_send, p_recv,
):
    x = lax.axis_index("gx")
    gy = lax.axis_index("gy")
    z = gy // 8
    y = (gy // 2) % 4
    c = gy % 2
    first = c == 0
    me = x * 32 + gy
    def along_x(core):
        return core == 0

    def pick(a, b):
        return jnp.where(along_x(c), a, b)

    v = pick(x, z)
    w = pick(z, x)

    def on_line(place, core):
        return (pick(place, x), pick(z, place) * 8 + y * 2 + core)

    def on_gather(place):
        return (pick(x, place), pick(place, z) * 8 + y * 2 + c)

    def ring(step):
        d = lax.rem(me + step + 128, 128)
        return (d // 32, lax.rem(d, 32))

    sibling = (x, z * 8 + y * 2 + 1 - c)
    y_dev = lambda k: (x, z * 8 + lax.rem(y + k, 4) * 2 + c)
    x_dev = lambda k, core: (lax.rem(x + k, 4), z * 8 + y * 2 + core)
    z_dev = lambda k, core: (x, lax.rem(z + k, 4) * 8 + y * 2 + core)

    def send(src, dst, send_sem, recv_sem, device):
        copy = pltpu.make_async_remote_copy(
            src_ref=src, dst_ref=dst, send_sem=send_sem, recv_sem=recv_sem,
            device_id=device, device_id_type=MESH,
        )
        copy.start()
        return copy

    def arrived(src, dst, send_sem, recv_sem):
        pltpu.make_async_remote_copy(
            src_ref=src, dst_ref=dst, send_sem=send_sem, recv_sem=recv_sem,
            device_id=sibling, device_id_type=MESH,
        ).wait_recv()

    loads = {}

    def load(name, src, dst):
        loads[name] = pltpu.make_async_copy(src, dst, load_sem.at[len(loads)])
        loads[name].start()

    load("rs", rs_hbm, rlo.at[pl.ds(8, 16)])
    load("cb", cb_hbm, cb)
    load("lu", lu_hbm, lu)
    load("mu", mu_hbm, mu)
    load("mb", mb_hbm, mb)
    load("md", md_hbm, md)

    barrier = pltpu.get_barrier_semaphore()
    peers = [sibling]
    for k in range(1, LINE):
        peers += [y_dev(k), x_dev(k, 0), x_dev(k, 1), z_dev(k, 0), z_dev(k, 1)]
    for peer in peers:
        pl.semaphore_signal(barrier, inc=1, device_id=peer, device_id_type=MESH)

    @pl.when(me > 0)
    def _():
        pl.semaphore_signal(barrier, inc=1, device_id=ring(-1), device_id_type=MESH)

    @pl.when(me < 127)
    def _():
        pl.semaphore_signal(barrier, inc=1, device_id=ring(1), device_id_type=MESH)

    expected = len(peers) + jnp.where(me > 0, 1, 0) + jnp.where(me < 127, 1, 0)

    def start_rest():
        load("rs2", rs_hbm, rhi.at[pl.ds(0, 16)])
        load("ns", ns_hbm, ns)
        load("nc", nc_hbm, nc)
        load("cs", cs_hbm, cs)
        load("cc", cc_hbm, cc)
        load("ts", ts_hbm, ts)
        load("ms", ms_hbm, msv.at[mine])
        load("cp", cp_hbm, cp)
        for place in range(LINE):
            load(f"tb{place}", tb_hbm.at[top_of(place)], tb.at[place])
        load("ld", ld_hbm, ld)
        load("rb", rb_hbm, rb)
        for t in range(16):
            pltpu.make_async_copy(nb_hbm.at[t], nb.at[t], nb_sem.at[t]).start()

    def top_of(place):
        return pick(place * 8 + z * 2, x * 8 + place * 2) + y // 2

    def skeletons():
        for l in range(16):
            skw[8 + l] = dot_nt(cb[l], rlo[8 + l]).astype(BF16)
        loads["mu"].wait()
        lift = None
        for m in range(2):
            raised = dot(ust[m], skw[8 + 8 * m : 16 + 8 * m].reshape(512, 128)).astype(BF16)
            mown[m] = raised
            lifted = dot(mu[m], raised).astype(BF16).astype(F32)
            lift = lifted if lift is None else lift + lifted
        mown[2] = lift.astype(BF16)

    def send_y():
        copies["y"] = [
            send(mown, g1.at[y], y_send.at[k - 1], y_recv.at[k - 1], y_dev(k)) for k in range(1, LINE)
        ]

    def send_skel():
        copies["skel"] = exchange(skw, skw, 24, skel_send, skel_recv)

    def send_halo():
        copies["halo"] = exchange(rlo, rhi, 16, halo_send, halo_recv)

    def exchange(window, above, at, send_sem, recv_sem):
        down = pltpu.make_async_remote_copy(
            src_ref=window.at[pl.ds(8, 8)], dst_ref=above.at[pl.ds(at, 8)],
            send_sem=send_sem.at[0], recv_sem=recv_sem.at[0], device_id=ring(-1), device_id_type=MESH,
        )
        up = pltpu.make_async_remote_copy(
            src_ref=window.at[pl.ds(16, 8)], dst_ref=window.at[pl.ds(0, 8)],
            send_sem=send_sem.at[1], recv_sem=recv_sem.at[1], device_id=ring(1), device_id_type=MESH,
        )
        pl.when(gy % 8 != 0)(down.start)
        pl.when(gy % 8 != 7)(up.start)
        return down, up

    def send_late(name):
        down, up = copies[name]
        pl.when(jnp.logical_and(gy % 8 == 0, me > 0))(down.start)
        pl.when(jnp.logical_and(gy % 8 == 7, me < 127))(up.start)

    def wait_window(name):
        down, up = copies[name]
        pl.when(me < 127)(down.wait_recv)
        pl.when(me > 0)(up.wait_recv)

    def stack_q():
        loads["mb"].wait()
        loads["md"].wait()
        for m in range(2):
            qown[:, 256 * m : 256 * m + 256] = jnp.concatenate([mb[m, k] for k in range(4)], axis=1)
        qown[:, 512:] = jnp.concatenate([md[0], md[1]], axis=1)

    def send_q():
        slot0, slot1 = x * 2 + c, z * 2 + c
        for k in range(1, LINE):
            for core in range(2):
                device = tuple(jnp.where(along_x(core), a, b) for a, b in zip(x_dev(k, core), z_dev(k, core)))
                slot = jnp.where(along_x(core), slot0, slot1)
                at = 2 * (k - 1) + core
                sem = 2 * (k - 1) + c
                sent.append(send(qown, qin.at[slot], q_send.at[at], q_recv.at[sem], device))
                sent.append(send(ms_hbm, msv.at[slot], i_send.at[at], i_recv.at[sem], device))
        slot = jnp.where(along_x(1 - c), slot0, slot1)
        sent.append(send(qown, qin.at[slot], q_send.at[6], q_recv.at[6], sibling))
        sent.append(send(ms_hbm, msv.at[slot], i_send.at[6], i_recv.at[6], sibling))
        qin[mine] = qown[...]

    def stack_t():
        for place in range(LINE):
            loads[f"tb{place}"].wait()
            tst[place] = jnp.concatenate([tb[place, k] for k in range(4)], axis=1)

    def send_g():
        g1[y] = mown[...]
        for copy in copies["y"]:
            copy.wait_recv()
        for p in range(4):
            for m in range(2):
                g2[w * PER + 2 * p + m] = g1[p, m]
        for h in range(2):
            g2[w * PER + 8 + h] = (g1[2 * h, 2].astype(F32) + g1[2 * h + 1, 2].astype(F32)).astype(BF16)
        half = PER // 2
        up, down = on_gather(lax.rem(w + 1, LINE)), on_gather(lax.rem(w + 3, LINE))
        low, high = g2.at[pl.ds(w * PER, half)], g2.at[pl.ds(w * PER + half, half)]
        copies["g"] = [
            send(part, part, g_send.at[at], g_recv.at[at], device)
            for at, (part, device) in enumerate(((low, up), (high, down), (high, up), (low, down)))
        ]

    def forward_g():
        half = PER // 2
        up, down = on_gather(lax.rem(w + 1, LINE)), on_gather(lax.rem(w + 3, LINE))
        for at, place, start, device in ((0, w + 3, 0, up), (1, w + 1, half, down)):
            copies["g"][at].wait_recv()
            part = g2.at[pl.ds(lax.rem(place, LINE) * PER + start, half)]
            copies["g"].append(send(part, part, g_send.at[4 + at], g_recv.at[4 + at], device))

    def stack_c():
        loads["cp"].wait()
        for t in range(16):
            cst[t] = jnp.concatenate([cp[t, k] for k in range(8)], axis=1)

    def couple():
        wait_window("skel")
        loads["cs"].wait()
        loads["cc"].wait()
        for t in range(16):
            rows = []
            for k in range(8):
                row = skw[jnp.clip(cs[k, t] - base, 0, 31)]
                rows.append(jnp.where(k < cc[t], row, jnp.zeros_like(row)))
            leaf_far[t] = dot(cst[t], jnp.concatenate(rows, axis=0))

    def fold():
        for at in range(7):
            arrived(qown, qin.at[0], q_send.at[at], q_recv.at[at])
            arrived(ms_hbm, msv.at[0], i_send.at[at], i_recv.at[at])
        loads["ms"].wait()
        loads["ts"].wait()
        tables = pltpu.make_async_copy(msv, mss, out_sem.at[0])
        tables.start()
        lane = lax.broadcasted_iota(jnp.int32, (64, 128), 1)
        for s in range(8):
            down = qin[s, :, 512:]
            zero = jnp.zeros_like(down)
            both = jnp.concatenate(
                [jnp.where(lane < 64, down, zero), jnp.where(lane < 64, zero, down)], axis=0
            )
            folded = dot(both, jnp.concatenate([tst[s // 2], tst[s // 2]], axis=0)).astype(BF16)
            for m in range(2):
                qfull[s, m, :, :256] = qin[s, :, 256 * m : 256 * m + 256]
                qfull[s, m, :, 256:] = folded[64 * m : 64 * m + 64]
        tables.wait()
        g2[LINE * PER] = jnp.zeros((64, 128), BF16)
        for i in range(4):
            for s in range(8):
                for m in range(2):
                    mix[s, m, i] = mid_at(mss[s, m, i])
            for place in range(LINE):
                tix[place, i] = top_at(ts[i, top_of(place)])

    def near(window, start, shift):
        def step(i, carry):
            t = start + i
            total = jnp.zeros((128, 256), F32)
            for k in range(8):
                side = window[jnp.clip(ns[k, t] - shift, 0, 23)]
                total += dot_nt(jnp.where(k < nc[t], side, jnp.zeros_like(side)), nb[t, k])
            acc[t] = total
            return carry

        lax.fori_loop(0, 8, step, 0)

    def near_low():
        pl.when(me > 0)(copies["halo"][1].wait_recv)
        near(rlo, 0, me * 16 - 8)

    def near_high():
        pl.when(me < 127)(copies["halo"][0].wait_recv)
        near(rhi, 8, me * 16)

    def near_fast():
        pl.when(first)(near_high)
        pl.when(c == 1)(near_low)

    def near_slow():
        pl.when(first)(near_low)
        pl.when(c == 1)(near_high)

    def wait_near():
        loads["rs2"].wait()
        loads["ns"].wait()
        loads["nc"].wait()
        for t in range(16):
            pltpu.make_async_copy(nb_hbm.at[t], nb.at[t], nb_sem.at[t]).wait()

    def mid_at(m):
        dev = m // 2
        mx, mz, my, mc = dev // 32, (dev // 8) % 4, (dev // 2) % 4, dev % 2
        held = (mc == c) & (pick(mx, mz) == v)
        return jnp.where(held, pick(mz, mx) * PER + my * 2 + m % 2, LINE * PER)

    def top_at(n):
        nx, nz = n // 8, (n // 2) % 4
        return jnp.where(pick(nx, nz) == v, pick(nz, nx) * PER + 8 + n % 2, LINE * PER)

    def serve():
        for copy in copies["g"][2:]:
            copy.wait_recv()
        for k in range(1, LINE + 1):
            place = lax.rem(v + k, LINE)
            tops = [g2[tix[place, i]] for i in range(4)]
            for core in range(2):
                s = 2 * place + core
                for m in range(2):
                    rows = [g2[mix[s, m, i]] for i in range(4)]
                    psend[s, m] = dot(qfull[s, m], jnp.concatenate(rows + tops, axis=0)).astype(BF16)
                if k < LINE:
                    at = 2 * (k - 1) + core
                    sent.append(
                        send(psend.at[s], precv.at[4 * c + v], p_send.at[at], p_recv.at[3 * c + k - 1],
                             on_line(place, core))
                    )
        sent.append(
            send(psend.at[2 * v + 1 - c], precv.at[4 * c + v], p_send.at[6], p_recv.at[6], sibling)
        )
        precv[4 * c + v] = psend[mine]

    def lower():
        loads["ld"].wait()
        loads["rb"].wait()
        for at in range(7):
            arrived(psend.at[0], precv.at[0], p_send.at[at], p_recv.at[at])
        for m in range(2):
            total = precv[0, m].astype(F32)
            for s in range(1, 8):
                total += precv[s, m].astype(F32)
            lowered = dot(ld[8 * m : 8 * m + 8].reshape(512, 64), total.astype(BF16))
            for l in range(8):
                t = 8 * m + l
                local = (leaf_far[t] + lowered[64 * l : 64 * l + 64]).astype(BF16)
                out[t] = (acc[t] + dot_tn(local, rb[t])).astype(BF16)

    def finish():
        for copy in sent + copies["y"] + copies["g"]:
            copy.wait_send()
        for name in ("skel", "halo"):
            down, up = copies[name]
            pl.when(me > 0)(down.wait_send)
            pl.when(me < 127)(up.wait_send)

    copies, sent = {}, []
    mine = 2 * v + c
    base = me * 16 - 8
    loads["lu"].wait()
    for m in range(2):
        ust[m] = jnp.concatenate([lu[8 * m + l] for l in range(8)], axis=1)
    loads["rs"].wait()
    loads["cb"].wait()
    start_rest()
    skeletons()
    pl.semaphore_wait(barrier, expected)
    send_y()
    send_halo()
    send_skel()
    send_late("skel")
    stack_q()
    send_q()
    stack_t()
    send_g()
    stack_c()
    forward_g()
    send_late("halo")
    fold()
    pl.when(z <= 2)(wait_near)
    pl.when(z <= 2)(near_fast)
    serve()
    pl.when(z > 2)(wait_near)
    pl.when(z > 2)(near_fast)
    near_slow()
    couple()
    lower()
    finish()


def local(*args):
    args = list(args)
    for at in (1, 7, 13):
        args[at] = args[at].T
    vmem = pltpu.VMEM
    smem = pltpu.SMEM
    dma = pltpu.SemaphoreType.DMA
    scratch = [
        vmem((24, 128, 256), BF16),
        vmem((24, 128, 256), BF16),
        vmem((16, 8, 256, 256), BF16),
        vmem((16, 64, 256), BF16),
        vmem((16, 64, 256), BF16),
        vmem((16, 64, 64), BF16),
        vmem((16, 8, 64, 64), BF16),
        vmem((2, 64, 64), BF16),
        vmem((2, 4, 64, 64), BF16),
        vmem((4, 4, 64, 64), BF16),
        vmem((2, 64, 64), BF16),
        vmem((16, 64, 64), BF16),
        smem((8, 16), jnp.int32),
        smem((16,), jnp.int32),
        smem((8, 16), jnp.int32),
        smem((16,), jnp.int32),
        smem((4, 32), jnp.int32),
        smem((8, 2, 4), jnp.int32),
        smem((8, 2, 4), jnp.int32),
        smem((4, 4), jnp.int32),
        vmem((8, 2, 4), jnp.int32),
        vmem((32, 64, 128), BF16),
        vmem((2, 64, 512), BF16),
        vmem((16, 64, 512), BF16),
        vmem((4, 64, 256), BF16),
        vmem((64, 640), BF16),
        vmem((8, 64, 640), BF16),
        vmem((8, 2, 64, 512), BF16),
        vmem((3, 64, 128), BF16),
        vmem((4, 3, 64, 128), BF16),
        vmem((4 * PER + 1, 64, 128), BF16),
        vmem((8, 2, 64, 128), BF16),
        vmem((8, 2, 64, 128), BF16),
        vmem((16, 64, 128), F32),
        vmem((16, 128, 256), F32),
        dma((20,)), dma((16,)), dma((1,)),
        dma((2,)), dma((2,)), dma((2,)), dma((2,)),
        dma((7,)), dma((7,)), dma((7,)), dma((7,)),
        dma((3,)), dma((3,)), dma((6,)), dma((6,)),
        dma((7,)), dma((7,)),
    ]
    return pl.pallas_call(
        kernel,
        out_shape=jax.ShapeDtypeStruct((16, 128, 256), BF16),
        in_specs=[pl.BlockSpec(memory_space=pl.ANY)] * len(args),
        out_specs=pl.BlockSpec(memory_space=pltpu.VMEM),
        scratch_shapes=scratch,
        compiler_params=pltpu.CompilerParams(
            collective_id=0, has_side_effects=True, vmem_limit_bytes=56 * 1024 * 1024
        ),
    )(*args)


def solution(mesh):
    both = ("gx", "gy")
    placed = [P(both)] * 17
    placed[13] = placed[14] = P()
    return jax.shard_map(
        local, mesh=mesh, in_specs=tuple(placed), out_specs=P(both), check_vma=False
    )
```

time: 40.2 us -> 37 us (0.920)
  the two profiles are of different devices: /device:TPU:1 before, /device:TPU:2 now
where the time goes in v2:
time: 37 us; the launch traced here: 36.9 us
  Pallas kernels  34.6 us (94%)
  local copies, waits for them, and re-layouts  2.29 us (6%)
    pallas_call x1, Pallas kernels, local(): pl.pallas_call(kernel, out_shape=jax.ShapeDtypeStruct((16, 128, 256), BF1...  34.6 us
    unnamed x1, local copies, waits for them, and re-layouts  2.29 us

profile of v2, /device:TPU:2, one launch (start us, length us, event | category | flops | bytes accessed | tf_op | source)
XLA Modules:
  0.0 36.9 jit_solution(8630658326196164997)
XLA Ops:
  0.0 34.6 %shard_map.163 = bf16[16,128,256]{2,1,0:T(8,128)(2,1)} custom-call(bf16[16,128,256]{2,1,0:T(8,128)(2,1)} %rs_hbm.1, s32[8,16]{1,0:T(8,128)} %bitcast.3, s32[16]{0:T(128)} %nc_hbm.1, bf16[16,8,256,256]{3,2,1,0:T(8,128)(2,1)} %nb_hbm.1, bf16[16,64,256]{2,1,0:T(8,128)(2,1)} %cb_hbm.1, bf16[16,64,256]{2,1,0:T(8,128)(2,1)} %rb_hbm.1, bf16[16,64,64]{2,1,0:T(8,128)(2,1)} %lu_hbm.1, ...), custom_call_target="tpu_custom_call" | custom-call | tf_op jit(solution)/shard_map/pallas_call | solution.py:450
  34.6 2.3 %copy.19 = bf16[16,128,256]{2,1,0:T(8,128)(2,1)} copy(bf16[16,128,256]{2,1,0:T(8,128)(2,1)} %shard_map.163) | data formatting | bytes 2097152

commit v3 on v2

--- a/solution.py
+++ b/solution.py
@@ -387,13 +387,11 @@
     forward_g()
     send_late("halo")
     fold()
-    pl.when(z <= 2)(wait_near)
-    pl.when(z <= 2)(near_fast)
+    wait_near()
+    near_fast()
     serve()
-    pl.when(z > 2)(wait_near)
-    pl.when(z > 2)(near_fast)
+    couple()
     near_slow()
-    couple()
     lower()
     finish()
 

time: 37 us -> 35.6 us (0.962)
  Pallas kernels: 34.6 us -> 33.1 us
    pallas_call x1, Pallas kernels: 34.6 us -> 33.1 us  [local(): pl.pallas_call(kernel, out_shape=jax.ShapeDtypeStruct((16, 128, 256), BF1...]
where the time goes in v3:
time: 35.6 us; the launch traced here: 35.4 us
  Pallas kernels  33.1 us (93%)
  local copies, waits for them, and re-layouts  2.29 us (6%)
    pallas_call x1, Pallas kernels, local(): pl.pallas_call(kernel, out_shape=jax.ShapeDtypeStruct((16, 128, 256), BF1...  33.1 us
    unnamed x1, local copies, waits for them, and re-layouts  2.29 us

profile of v3, /device:TPU:2, one launch (start us, length us, event | category | flops | bytes accessed | tf_op | source)
XLA Modules:
  0.0 35.4 jit_solution(6036584895923635604)
XLA Ops:
  0.0 33.1 %shard_map.163 = bf16[16,128,256]{2,1,0:T(8,128)(2,1)} custom-call(bf16[16,128,256]{2,1,0:T(8,128)(2,1)} %rs_hbm.1, s32[8,16]{1,0:T(8,128)} %bitcast.3, s32[16]{0:T(128)} %nc_hbm.1, bf16[16,8,256,256]{3,2,1,0:T(8,128)(2,1)} %nb_hbm.1, bf16[16,64,256]{2,1,0:T(8,128)(2,1)} %cb_hbm.1, bf16[16,64,256]{2,1,0:T(8,128)(2,1)} %rb_hbm.1, bf16[16,64,64]{2,1,0:T(8,128)(2,1)} %lu_hbm.1, ...), custom_call_target="tpu_custom_call" | custom-call | tf_op jit(solution)/shard_map/pallas_call | solution.py:448
  33.1 2.3 %copy.19 = bf16[16,128,256]{2,1,0:T(8,128)(2,1)} copy(bf16[16,128,256]{2,1,0:T(8,128)(2,1)} %shard_map.163) | data formatting | bytes 2097152
